TPU v7x, 32 devices: a whole 2x2x4 slice. The times are simulated.
32 devices in a mesh: section: 2 (over core), dp: 16 (over z, y, x).
Axes of the slice: x: 2, y: 2, z: 4, core: 2. Of those that a mesh axis runs over, the one named last changes fastest.
Arguments:
- tokens: bfloat16 [2, 10240, 768], P(None, 'dp'), may hold values from -6 to 6
- lengths: int32 [2, 16, 8], P(None, 'dp'), may hold values from 20 to 197, as said below
- route_mask: int32 [2, 10240], P(None, 'dp'), may hold values from 0 to 1, as said below
- router_weight: bfloat16 [768], replicated, may hold values from -0.21875 to 0.21875
- gains: float32 [2, 1536], P('section'), may hold values from 0.5 to 1.5
- biases: float32 [2, 7680], P('section'), may hold values from -2 to 2
- w_qkv: bfloat16 [2, 768, 2304], P('section'), may hold values from -0.21875 to 0.21875
- w_out: bfloat16 [2, 768, 768], P('section'), may hold values from -0.625 to 0.625
- w_up: bfloat16 [2, 768, 3072], P('section'), may hold values from -0.21875 to 0.21875
- w_down: bfloat16 [2, 3072, 768], P('section'), may hold values from -0.109375 to 0.109375
- cotangent: bfloat16 [2, 10240, 768], P(None, 'dp'), may hold values from -6 to 6
Outputs:
- activations: bfloat16 [2, 2, 10240, 768], P('section', None, 'dp')
- input_grads: bfloat16 [2, 2, 10240, 768], P('section', None, 'dp')
- grad_qkv: float32 [2, 768, 2304], P('section')
- grad_out: float32 [2, 768, 768], P('section')
- grad_up: float32 [2, 768, 3072], P('section')
- grad_down: float32 [2, 3072, 768], P('section')
- grad_gains: float32 [2, 1536], P('section')
- grad_biases: float32 [2, 7680], P('section')
- grad_router: float32 [768], replicated
- router_score_mean: float32 [2], replicated
Inputs may be any that keep to these rules, and one draw needn't show every extreme that they name: In each device's block the 8 lengths sum to 640: two are 197, the other six form three pairs that each sum to 82, in a drawn order. `route_mask`: in every crop exactly half of the positions, rounded down, are 1.
All inputs are finite; a program needn't handle non-finite values.
Results may differ from a plain program's by a relative error of at most 0.015.
Values may be sent and summed in bfloat16 or wider, within the bound.
A program may use at most 256 MiB of HBM per device.

v0:
```python
import functools

import jax
import jax.numpy as jnp
from jax import lax
from jax.experimental import pallas as pl
from jax.experimental.pallas import tpu as pltpu
from jax.sharding import PartitionSpec as P

HEADS = 12
HEAD = 64
LONG = 197
F32 = jnp.float32
BF16 = jnp.bfloat16
NT = (((1,), (1,)), ((), ()))
TN = (((0,), (0,)), ((), ()))
NN = (((1,), (0,)), ((), ()))


LANES = 768
TILE = 16
GRAD_ROWS = 12 * LANES


def axis_bits(mesh):
    line = mesh.devices[0]
    bits = len(line).bit_length() - 1
    try:
        spots = [tuple(device.coords) for device in line]
    except AttributeError:
        return [0] * bits
    return [
        next((w for w in range(3) if spots[1 << b][w] != spots[0][w]), 0) for b in range(bits)
    ]


HALVINGS = 4
GROUPS = 6
SLOTS = 4


GROUP_PLAN = (
    ((768, 1023), (768, 132)),
    ((768, 123), (512, 1023), (256, 1203)),
    ((768, 123), (768, 1032)),
    ((512, 2103), (512, 123), (512, 1032)),
    ((768, 1023), (512, 2103), (256, 132)),
    ((512, 2013), (512, 132), (512, 1203)),
)
REDUCED = ((0, 3), (2, 1))
GROUP_STARTS = (0, 1, 2, 4, 5, 7)


def sum_plan(axis_of):
    lists = {}
    for bit, axis in enumerate(axis_of):
        lists.setdefault(axis, []).append(bit)
    lists = sorted(lists.values(), key=len)
    while len(lists) < 3:
        lists.append([])
    roles = [lists[0][:1], lists[1][:1], lists[2][:1], lists[2][1:2]]
    plan = []
    for group in GROUP_PLAN:
        chunks, start = [], 0
        for size, code in group:
            order = [bit for place in (1000, 100, 10, 1) for bit in roles[code // place % 10]]
            order += [bit for bit in range(len(axis_of)) if bit not in order]
            chunks.append((start, size, order))
            start += size
        plan.append(chunks)
    return plan


def add_rows(into, into_start, source, start, other, other_start, count):
    tile = next(t for t in (64, 32, 16) if count % t == 0)

    def step(k, carry):
        target, here, there = (
            pl.ds(pl.multiple_of(first + k * tile, TILE), tile) for first in (into_start, start, other_start)
        )
        into[target, :] = source[here, :] + other[there, :]
        return carry

    lax.fori_loop(0, count // tile, step, 0)


class Names:
    pass


def copy_far(source, target, one, two, friend):
    return pltpu.make_async_remote_copy(
        src_ref=source,
        dst_ref=target,
        send_sem=one,
        recv_sem=two,
        device_id=friend,
        device_id_type=pl.DeviceIdType.MESH,
    )


def at_core(core, index, step):
    pl.when(core == index)(step)


GRAD_TILES = 36
GROUP_ROWS = GRAD_ROWS // GROUPS


class Sums:
    def __init__(self, chunks, jobs, tiles, given, whole):
        self.chunks, self.jobs, self.tiles = chunks, jobs, tiles
        self.bits = bits = len(chunks[0][0][2])
        self.halvings = min(bits, HALVINGS)
        self.acc, self.mate = next(given), next(given)
        self.got = [next(given) for _ in range(bits)]
        self.load_sem, self.mate_sem = (next(given) for _ in range(2))
        self.send, self.recv, self.back_send, self.back_recv = (next(given) for _ in range(4))
        self.tile_recv, self.ready = (next(given) for _ in range(2))
        if whole:
            self.small_got, self.small = next(given), next(given)
            self.small_send, self.small_recv = (next(given) for _ in range(2))
            self.shown_sem, self.shown_send, self.shown_recv = (next(given) for _ in range(3))
            self.give_send, self.give_recv, self.put_sem = (next(given) for _ in range(3))
        self.core = lax.axis_index("section")
        self.me = lax.axis_index("dp")
        self.across = (1 - self.core, self.me)
        self.end = max(start + last - first + 1 for start, first, last in jobs.values())
        self.now = 0

    @staticmethod
    def scratch(chunks, held_groups, small_rows):
        bits = len(chunks[0][0][2])
        count = sum(len(group) for group in chunks)
        rows = min(held_groups, SLOTS) * GROUP_ROWS
        held = [pltpu.VMEM((held_groups * GROUP_ROWS, LANES), BF16), pltpu.VMEM((GROUP_ROWS, LANES), BF16)]
        held += [pltpu.VMEM((rows >> min(depth + 1, HALVINGS), LANES), BF16) for depth in range(bits)]
        held += [pltpu.SemaphoreType.DMA((count,))] * 2
        held += [pltpu.SemaphoreType.DMA((count, bits))] * 4
        held += [pltpu.SemaphoreType.DMA((GRAD_TILES,))]
        held += [pltpu.SemaphoreType.REGULAR((count, min(bits, HALVINGS)))]
        if small_rows:
            held += [pltpu.VMEM((bits + 1, small_rows, LANES), F32), pltpu.VMEM((2, small_rows, LANES), F32)]
            held += [pltpu.SemaphoreType.DMA((bits + 1,))] * 2
            held += [pltpu.SemaphoreType.DMA((2,))] * 3
            held += [pltpu.SemaphoreType.DMA((GROUPS,))] * 3
        return held

    def bit_at(self, bit):
        return lax.rem(self.me // (1 << bit), 2)

    def partner(self, bit):
        return (self.core, self.me + (1 - 2 * self.bit_at(bit)) * (1 << bit))

    def open(self):
        friends = [self.across] + [self.partner(bit) for bit in range(self.bits)]
        barrier = pltpu.get_barrier_semaphore()
        for friend in friends:
            pl.semaphore_signal(barrier, inc=1, device_id=friend, device_id_type=pl.DeviceIdType.MESH)
        pl.semaphore_wait(barrier, len(friends))

    @staticmethod
    def layer_of(j):
        return 1 if j < GROUPS // 2 else 0

    def base(self, j, core):
        return (2 * (j % (GROUPS // 2)) + core) * GROUP_ROWS

    def rows_at(self, j, core, c):
        start, size, _ = self.chunks[j][c]
        return pl.ds(pl.multiple_of(self.base(j, core) + start, TILE), size)

    def index(self, j, c):
        return sum(len(group) for group in self.chunks[:j]) + c

    def load(self, j, c):
        start, size, _ = self.chunks[j][c]
        target = self.acc.at[pl.ds(j * GROUP_ROWS + start, size), :]
        source = self.grads[self.layer_of(j)].at[self.rows_at(j, self.core, c), :]
        return pltpu.make_async_copy(source, target, self.load_sem.at[self.index(j, c)])

    def load_mate(self, j, c):
        source = self.landed[self.layer_of(j)].at[self.rows_at(j, self.core, c), :]
        start, size, _ = self.chunks[j][c]
        target = self.mate.at[pl.ds(start, size), :]
        return pltpu.make_async_copy(source, target, self.mate_sem.at[self.index(j, c)])

    def span(self, j, c, depth):
        start, size, order = self.chunks[j][c]
        for bit in order[: min(depth, self.halvings)]:
            size //= 2
            start = start + self.bit_at(bit) * size
        return start, size

    def in_acc(self, j, start, size):
        return pl.ds(pl.multiple_of(j * GROUP_ROWS + start, TILE), size)

    def got_at(self, j, c, depth):
        return (j % SLOTS * GROUP_ROWS + self.chunks[j][c][0]) >> min(depth + 1, HALVINGS)

    def down(self, j, c, depth):
        bit = self.chunks[j][c][2][depth]
        start, size = self.span(j, c, depth)
        if depth < self.halvings:
            size //= 2
            start = start + (1 - self.bit_at(bit)) * size
        k = self.index(j, c)
        return copy_far(
            self.acc.at[self.in_acc(j, start, size), :],
            self.got[depth].at[pl.ds(self.got_at(j, c, depth), size), :],
            self.send.at[k, depth],
            self.recv.at[k, depth],
            self.partner(bit),
        )

    def up(self, j, c, depth):
        bit = self.chunks[j][c][2][depth]
        start, size = self.span(j, c, depth + 1)
        here = self.acc.at[self.in_acc(j, start, size), :]
        k = self.index(j, c)
        return copy_far(here, here, self.back_send.at[k, depth], self.back_recv.at[k, depth], self.partner(bit))

    def left(self, j, c, depth):
        self.down(j, c, depth).wait_send()
        if self.jobs[j][2] > self.bits:
            partner = self.partner(self.chunks[j][c][2][depth])
            pl.semaphore_signal(
                self.ready.at[self.index(j, c), depth], inc=1, device_id=partner, device_id_type=pl.DeviceIdType.MESH
            )

    def raise_up(self, j, c, depth):
        if depth >= self.jobs[j][1]:
            pl.semaphore_wait(self.ready.at[self.index(j, c), depth], 1)
        self.up(j, c, depth).start()

    def carried(self, j, c, keep):
        start, size = self.span(j, c, REDUCED[j][1])
        here = self.in_acc(j, start, size)
        pair = (self.acc.at[here, :], self.carry.at[here, :])
        return pltpu.make_async_copy(*(pair if keep else pair[::-1]), self.load_sem.at[self.index(j, c)])

    def wait_tiles(self, layer, first):
        for tile in range(6):
            area = self.landed[layer].at[pl.ds(0, LANES), pl.ds(0, STEP)]
            sem = self.tile_recv.at[first + self.core * 6 + tile]
            copy_far(area, area, sem, sem, self.across).wait_recv()

    def tile_out(self, layer, stage, row, column, shape, sem, tile):
        area = (pl.ds(row, shape[0]), pl.ds(column, shape[1]))
        owner = lax.rem(tile // 6, 2)

        @pl.when(self.core == owner)
        def _():
            pltpu.make_async_copy(stage, self.grads[layer].at[area], sem).start()

        @pl.when(self.core != owner)
        def _():
            copy_far(stage, self.landed[layer].at[area], sem, self.tile_recv.at[tile], self.across).start()

    def give(self, j, core):
        rows = pl.ds(self.base(j, core), GROUP_ROWS)
        source = self.acc.at[pl.ds(j * GROUP_ROWS, GROUP_ROWS), :]
        target = self.full[self.layer_of(j)].at[rows, :]
        return copy_far(source, target, self.give_send.at[j], self.give_recv.at[j], self.across)

    def put(self, j, core):
        rows = pl.ds(self.base(j, core), GROUP_ROWS)
        source = self.acc.at[pl.ds(j * GROUP_ROWS, GROUP_ROWS), :]
        return pltpu.make_async_copy(source, self.full[self.layer_of(j)].at[rows, :], self.put_sem.at[j])

    def each(self, j):
        return range(len(self.chunks[j]))

    def prepare(self, j):
        for c in self.each(j):
            self.load(j, c).start()
        if j in self.tiles:
            self.wait_tiles(self.layer_of(j), self.tiles[j])
        for c in self.each(j):
            self.load_mate(j, c).start()

    def moment(self):
        now, self.now = self.now, self.now + 1
        bits, halvings = self.bits, self.halvings
        order = sorted(self.jobs, key=lambda j: self.jobs[j][:2] != (now, 0))
        for j in order:
            start, first_stage, last_stage = self.jobs[j]
            stage = now - start + first_stage
            if not first_stage <= stage <= last_stage:
                continue
            for c in self.each(j):
                if stage == 0:
                    self.load(j, c).wait()
                    self.load_mate(j, c).wait()
                    first, size, _ = self.chunks[j][c]
                    at = j * GROUP_ROWS + first
                    add_rows(self.acc, at, self.acc, at, self.mate, first, size)
                    self.down(j, c, 0).start()
                elif stage == first_stage:
                    self.carried(j, c, False).wait()
                    self.down(j, c, stage).start()
                elif stage <= bits:
                    depth = stage - 1
                    if depth < halvings:
                        self.down(j, c, depth).wait_recv()
                        self.left(j, c, depth)
                    else:
                        self.down(j, c, depth).wait()
                    first, size = self.span(j, c, stage)
                    at = j * GROUP_ROWS + first
                    add_rows(self.acc, at, self.acc, at, self.got[depth], self.got_at(j, c, depth), size)
                    if stage < min(bits, last_stage):
                        self.down(j, c, stage).start()
                    elif stage < last_stage:
                        self.raise_up(j, c, halvings - 1)
                else:
                    depth = bits + halvings - stage
                    self.up(j, c, depth).wait_recv()
                    if depth > 0:
                        self.raise_up(j, c, depth - 1)
            if stage == bits + halvings:
                layer = self.layer_of(j)
                at_core(self.core, layer, lambda j=j, layer=layer: self.put(j, layer).start())
                at_core(self.core, 1 - layer, lambda j=j, layer=layer: self.give(j, 1 - layer).start())
        for j, (start, first_stage, _) in self.jobs.items():
            if start == now + 1 and first_stage == 0:
                self.prepare(j)

    def small_step(self, k):
        friend = self.across if k == 0 else self.partner(k - 1)
        return copy_far(
            self.small_out, self.small_got.at[k], self.small_send.at[k], self.small_recv.at[k], friend
        )

    def small_begin(self):
        for layer in range(2):

            def step(layer=layer):
                self.small_out[...] = self.small[layer]
                copy_far(
                    self.small.at[1 - layer], self.small_got.at[0], self.small_send.at[0], self.small_recv.at[0],
                    self.across,
                ).start()

            at_core(self.core, layer, step)

    def small_turn(self, k):
        self.small_step(k).wait()
        self.small_out[...] = self.small_out[...] + self.small_got[k]
        if k < self.bits:
            self.small_step(k + 1).start()

    def shown_keep(self, layer, k):
        return pltpu.make_async_copy(self.shown[2 * k + layer], self.shown_out[k].at[self.core], self.shown_sem.at[k])

    def shown_give(self, layer, k):
        return copy_far(
            self.shown[2 * k + 1 - layer], self.shown_out[k].at[self.core], self.shown_send.at[k],
            self.shown_recv.at[k], self.across,
        )

    def show(self):
        for layer in range(2):

            def step(layer=layer):
                for k in range(2):
                    self.shown_keep(layer, k).start()
                    self.shown_give(layer, k).start()

            at_core(self.core, layer, step)

    def close(self):
        for k in range(2):
            self.shown_keep(0, k).wait()
            self.shown_give(0, k).wait()
        for j in range(GROUPS):
            layer = self.layer_of(j)

            def kept(j=j, layer=layer):
                self.put(j, layer).wait()
                self.give(j, 1 - layer).wait_recv()

            at_core(self.core, layer, kept)
            at_core(self.core, 1 - layer, lambda j=j, layer=layer: self.give(j, 1 - layer).wait_send())
            for c in self.each(j):
                for depth in range(self.halvings):
                    self.up(j, c, depth).wait_send()


def cast_kernel(first, second, small, acts, slopes, qkv, out, up, down, *refs):
    gains, biases, router, means, acts_out, slopes_out, low, high, bounce, in_sem, out_sem, copy_sem = refs
    rows = low.shape[1]
    per = LANES // rows
    slots = low.shape[0]
    count = 12 * per
    core = lax.axis_index("section")
    passed = [
        (
            pltpu.make_async_copy(source, bounce.at[k], copy_sem.at[k]),
            pltpu.make_async_copy(bounce.at[k], target.at[0], copy_sem.at[k]),
        )
        for k, (source, target) in enumerate(((acts, acts_out), (slopes, slopes_out)))
    ]

    def take(k, source=first):
        return pltpu.make_async_copy(source.at[pl.ds(k * rows, rows), :], low.at[k % slots], in_sem.at[k % slots])

    def give(k):
        block, part = divmod(k, per)
        if block < 4:
            target = down.at[0, pl.ds(k * rows, rows), :]
        elif block < 8:
            target = up.at[0, pl.ds(part * rows, rows), pl.ds((block - 4) * LANES, LANES)]
        elif block < 9:
            target = out.at[0, pl.ds(part * rows, rows), :]
        else:
            target = qkv.at[0, pl.ds(part * rows, rows), pl.ds((block - 9) * LANES, LANES)]
        return pltpu.make_async_copy(high.at[k % slots], target, out_sem.at[k % slots])

    def fetch(k):
        at_core(core, 0, lambda: take(k).start())
        at_core(core, 1, lambda: take(k, second).start())

    for k in range(slots):
        fetch(k)
    for copy, _ in passed:
        copy.start()
    held = gains.shape[1] // LANES
    for row in range(held):
        gains[:, row * LANES : (row + 1) * LANES] = small[row : row + 1, :]
    for row in range(biases.shape[1] // LANES):
        biases[:, row * LANES : (row + 1) * LANES] = small[held + row : held + row + 1, :]
    row = held + biases.shape[1] // LANES
    router[...] = small[row : row + 1, :]
    micro = means.shape[1]
    means[...] = small[row + 1 : row + 2, :micro] / small[row + 1 : row + 2, micro : 2 * micro]
    for k in range(count):
        take(k).wait()
        if k >= slots:
            give(k - slots).wait()
        high[k % slots] = low[k % slots].astype(F32)
        give(k).start()
        if k + slots < count:
            fetch(k + slots)
        if k < 2:
            passed[k][0].wait()
            passed[k][1].start()
    for k in range(count - slots, count):
        give(k).wait()
    for _, copy in passed:
        copy.wait()


def cast_sums(sums, small, acts, slopes, shapes, micro):
    anywhere = pl.BlockSpec(memory_space=pl.ANY)
    inside = pl.BlockSpec(memory_space=pltpu.VMEM)
    outs = [(shape, F32) for shape in shapes] + [((1, LANES), F32), ((1, micro), F32)]
    outs += [((1, *value.shape), BF16) for value in (acts, slopes)]
    return pl.pallas_call(
        cast_kernel,
        out_shape=[jax.ShapeDtypeStruct(*one) for one in outs],
        in_specs=[anywhere] * 2 + [inside] + [anywhere] * 2,
        out_specs=[anywhere] * 4 + [inside] * 4 + [anywhere] * 2,
        scratch_shapes=[
            pltpu.VMEM((4, LANES, LANES), BF16),
            pltpu.VMEM((4, LANES, LANES), F32),
            pltpu.VMEM((2, *acts.shape), BF16),
            pltpu.SemaphoreType.DMA((4,)),
            pltpu.SemaphoreType.DMA((4,)),
            pltpu.SemaphoreType.DMA((2,)),
        ],
        compiler_params=pltpu.CompilerParams(vmem_limit_bytes=60 * 1024 * 1024),
        cost_estimate=pl.CostEstimate(flops=0, bytes_accessed=50 * 10**6, transcendentals=0),
        name="cast",
    )(*sums, small, acts, slopes)


STEP = 256
NEGATIVE = -1e30


def dot(left, right, dims=NN):
    return lax.dot_general(left, right, dims, preferred_element_type=F32)


def gelu_parts(pre):
    bell = jnp.exp(pre * pre * -0.5)
    t = pl.reciprocal(1.0 + jnp.abs(pre) * (0.3275911 * 0.7071067811865476))
    poly = t * (0.1274147960 + t * (-0.142248368 + t * (0.710706871 + t * (-0.7265760135 + t * 0.5307027145))))
    tail = poly * bell
    return jnp.where(pre >= 0.0, 1.0 - tail, tail), bell


def norm_stats(values):
    centred = values - jnp.mean(values, axis=-1, keepdims=True)
    recip = lax.rsqrt(jnp.mean(centred * centred, axis=-1, keepdims=True) + 1e-06)
    return centred * recip, recip


def fold(tile):
    return jnp.sum(tile.reshape(tile.shape[0] // 8, 8, tile.shape[1]), axis=0)


def front_names(r, given, full):
    r.weights = [next(given) for _ in range(4)]
    r.w_sem, r.n1, r.qkv, r.probs, r.mask, r.mix, r.between, r.n2, r.act = (next(given) for _ in range(9))
    if not full:
        r.pre = [next(given) for _ in range(2)]
    r.act_part = [next(given) for _ in range(2)]


def back_names(r, given, scaled):
    r.n1t, r.n2t = (next(given) for _ in range(2))
    r.mixt = r.n2t
    r.dmlp = next(given) if scaled else r.dout
    r.dpre, r.dn = (next(given) for _ in range(2))
    r.pre = [r.dn.at[:, pl.ds(side * STEP, STEP)] for side in range(2)]
    r.dqkv = r.dpre.at[:, pl.ds(0, 3 * LANES)]
    r.datt, r.dmix = r.n1, r.mix
    r.dpre_part = [next(given) for _ in range(2)]
    r.down_stage, r.up_stage, r.down_sem, r.up_sem = (next(given) for _ in range(4))


def use_weights(r, layer):
    core = lax.axis_index("section")

    def weight(which, source):
        return pltpu.make_async_copy(source[which].at[0], r.weights[which], r.w_sem.at[which])

    for near, source in ((core == layer, r.own), (core != layer, r.far)):

        @pl.when(near)
        def _():
            for which in range(4):
                weight(which, source).start()

    r.ready = lambda which: weight(which, r.own).wait()


def layer_kernel(groups, window, chunks, *refs):
    r = Names()
    given = iter(refs)
    r.x, r.col_code, r.row_code, r.vec = (next(given) for _ in range(4))
    r.own = [next(given) for _ in range(4)]
    r.far = [next(given) for _ in range(4)]
    r.unsort, r.dout = (next(given) for _ in range(2))
    r.shown_du, r.small, r.grads, r.du, r.shown_y, landed, carry = (next(given) for _ in range(7))
    front_names(r, given, True)
    back_names(r, given, False)
    r.y, r.shown_sem = r.n2, next(given)
    jobs = {j: (start, 0, stage) for j, (start, stage) in enumerate(REDUCED)}
    sums = Sums(chunks, jobs, {0: 0, 1: 12}, given, False)
    sums.grads, sums.landed, sums.carry = (None, r.grads), (None, landed), carry
    use_weights(r, 1)
    sums.open()
    r.tile_out = functools.partial(sums.tile_out, 1)
    r.hooks = {at: sums.moment for at in (4, 7, 8)}
    r.hooks[3] = lambda: sums.prepare(0)
    layer_body(r, groups, window, True, False)
    while sums.now < sums.end:
        sums.moment()
    for j in jobs:
        for c in sums.each(j):
            sums.carried(j, c, True).start()
    sums.wait_tiles(1, 24)
    for j in jobs:
        for c in sums.each(j):
            sums.carried(j, c, True).wait()


def start_kernel(groups, window, *refs):
    r = Names()
    given = iter(refs)
    lengths, route_mask, tokens, cotangent, router, own_vec = (next(given) for _ in range(6))
    own = [next(given) for _ in range(4)]
    far = [next(given) for _ in range(4)]
    vecs = [next(given) for _ in range(2)]
    r.all_y, r.shown_y, r.delta, cot, r.x = (next(given) for _ in range(5))
    col_codes = [next(given) for _ in range(2)]
    row_codes = [next(given) for _ in range(2)]
    r.unsort, pick, r.unpick, r.skipped, r.scale, factor, extra = (next(given) for _ in range(7))
    front_names(r, given, False)
    r.y, r.all_x, order, raw, far_vec, raw_sem = (next(given) for _ in range(6))
    far_send, far_recv, vec_sem = (next(given) for _ in range(3))
    core = lax.axis_index("section")
    across = (1 - core, lax.axis_index("dp"))
    rows, width = r.all_x.shape
    half = rows // 2

    def fetch(k, source):
        return pltpu.make_async_copy(source.at[core], raw.at[k], raw_sem.at[k])

    fetch(0, tokens).start()
    fetch(1, cotangent).start()
    barrier = pltpu.get_barrier_semaphore()
    pl.semaphore_signal(barrier, inc=1, device_id=across, device_id_type=pl.DeviceIdType.MESH)
    pl.semaphore_wait(barrier, 1)

    def lend(which):
        return copy_far(own[which], far[which], far_send.at[which], far_recv.at[which], across)

    lend_vec = copy_far(own_vec, far_vec, vec_sem.at[0], vec_sem.at[1], across)
    lend_vec.start()
    lend(0).start()

    def weight(which, source):
        return pltpu.make_async_copy(source[which].at[0], r.weights[which], r.w_sem.at[which])

    def take_own():
        for which in range(4):
            weight(which, own).start()

    at_core(core, 0, take_own)

    def ready(which):
        def arrive():
            lend(which).wait_recv()
            weight(which, far).start()

        at_core(core, 1, arrive)
        weight(which, own).wait()

    r.ready = ready

    starts, bases, total, longs, short = [], [], 0, 0, 0
    count = lengths.shape[2]
    sizes = [lengths[core, 0, c] for c in range(count)]
    for size in sizes:
        is_long = size == LONG
        starts.append(total)
        bases.append(jnp.where(is_long, longs * LONG, 2 * LONG + short))
        total = total + size
        longs = longs + jnp.where(is_long, 1, 0)
        short = short + jnp.where(is_long, 0, size)

    def place(shape, dim):
        return lax.broadcasted_iota(jnp.int32, shape, dim)

    def target(at):
        moved = at
        for start, size, base in zip(starts, sizes, bases):
            moved = moved + jnp.where((at >= start) & (at < start + size), base - start, 0)
        return moved

    def code_of(at):
        return sum(jnp.where(at >= base, 1, 0) for base in bases)

    row_at, col_at = place((1, rows), 1), place((rows, 1), 0)

    def one_hot(left, right):
        return jnp.where(left == right, 1.0, 0.0).astype(BF16)

    goes_row, goes_col = target(row_at), target(col_at)
    row_codes[1][...] = code_of(row_at)
    col_codes[1][...] = code_of(col_at)
    for start in range(0, rows, 128):
        here = slice(start, start + 128)
        order[here, :] = one_hot(col_at[here], goes_row)
        r.unsort[here, :] = one_hot(goes_col[here], row_at)
    lend(1).start()
    lend(2).start()
    lend(3).start()
    for k, (source, moved) in enumerate(((tokens, r.all_x), (cotangent, cot))):
        fetch(k, source).wait()
        moved[...] = dot(order[...], raw[k]).astype(BF16)

    mask = jnp.where(route_mask[pl.ds(core, 1), :] == 1, 1.0, 0.0)
    masks = jnp.broadcast_to(mask, (8, rows)).astype(BF16)
    chosen_row = dot(masks, r.unsort[...])
    chosen_col = dot(order[...], masks, NT)
    earlier = jnp.where(place((rows, rows), 0) < place((rows, rows), 1), 1.0, 0.0).astype(BF16)
    rank_row = dot(chosen_row.astype(BF16), earlier)[:1]
    later = jnp.where(place((rows, rows), 0) > place((rows, rows), 1), 1.0, 0.0).astype(BF16)
    rank_col = dot(later, chosen_col.astype(BF16))[:, :1]
    chosen_row, chosen_col = chosen_row[:1], chosen_col[:, :1]
    r.skipped[...] = 1.0 - chosen_col
    key_row = jnp.where(chosen_row > 0.5, rank_row, -1.0)
    key_col = jnp.where(chosen_col > 0.5, rank_col, -1.0)
    pick[...] = one_hot(place((half, 1), 0).astype(F32), key_row)
    r.unpick[...] = one_hot(key_col, place((1, half), 1).astype(F32))
    names_row = jnp.broadcast_to(code_of(row_at).astype(F32), (8, rows)).astype(BF16)
    routed_row = dot(names_row, r.unpick[...])[:1]
    routed_col = dot(pick[...], names_row, NT)[:, :1]
    row_codes[0][...] = routed_row.astype(jnp.int32)
    col_codes[0][...] = routed_col.astype(jnp.int32)
    r.x[...] = dot(pick[...], r.all_x[...]).astype(BF16)
    logit = jnp.sum(r.x[...].astype(F32) * router[...], axis=1, keepdims=True)
    gate = 1.0 / (1.0 + jnp.exp(-logit))
    held = jnp.where(routed_col > 0.5, 1.0, 0.0)
    r.scale[...] = held * gate
    factor[...] = held * gate * (1.0 - gate)
    gates, counts = jnp.sum(held * gate, axis=0, keepdims=True), jnp.sum(mask, axis=1, keepdims=True)
    lane = place((1, width), 1)
    micro = tokens.shape[0]
    extra[...] = jnp.where(lane == core, gates, jnp.where(lane == core + micro, counts, 0.0))

    lend_vec.wait()
    for layer in range(2):
        vecs[layer][...] = jnp.where(core == layer, own_vec[...], far_vec[...])
    r.vec, r.col_code, r.row_code, r.own = vecs[0], col_codes[0], row_codes[0], own
    r.hooks = {}
    layer_body(r, groups, window, False, True)
    for which in range(4):
        lend(which).wait_send()
        at_core(core, 0, lambda which=which: lend(which).wait_recv())


def fused_kernel(groups, window, chunks, *refs):
    r = Names()
    given = iter(refs)
    r.x, r.col_code, r.row_code, r.vec, r.scale = (next(given) for _ in range(5))
    r.own = [next(given) for _ in range(4)]
    r.far = [next(given) for _ in range(4)]
    r.unsort = next(given)
    r.all_dout, r.pick, r.unpick, r.skipped, r.delta, r.factor, r.router = (next(given) for _ in range(7))
    second, second_landed, carry, second_small, extra = (next(given) for _ in range(5))
    shown = [next(given) for _ in range(3)]
    full = [next(given) for _ in range(2)]
    first_landed, first, small_out = (next(given) for _ in range(3))
    shown_out = [next(given) for _ in range(2)]
    front_names(r, given, True)
    back_names(r, given, True)
    r.dout, r.du, r.shown_du, r.small, r.router_grad = (next(given) for _ in range(5))
    bits = len(chunks[0][0][2])
    last = bits + min(bits, HALVINGS)
    reduced = len(REDUCED)
    jobs = {j: (start, REDUCED[j][1] if j < reduced else 0, last) for j, start in enumerate(GROUP_STARTS)}
    sums = Sums(chunks, jobs, {3: 0, 4: 12, 5: 24}, given, True)
    sums.grads, sums.landed, sums.full = (first, second), (first_landed, second_landed), full
    sums.carry, sums.small_out = carry, small_out
    sums.shown, sums.shown_out = (shown[0], shown[1], r.shown_du, shown[2]), shown_out
    r.grads = first
    use_weights(r, 0)
    sums.open()
    for j in range(reduced):
        for c in sums.each(j):
            sums.carried(j, c, False).start()
    for j, (start, first_stage, _) in jobs.items():
        if start == 0 and first_stage == 0:
            sums.prepare(j)
    r.tile_out = functools.partial(sums.tile_out, 0)
    r.hooks = {at: sums.moment for at in (0, 1, 2, 3, 8, 9)}
    layer_body(r, groups, window, True, True)

    for index, source in enumerate((r.small, second_small)):
        for row in range(source.shape[1] // LANES):
            sums.small[index, row : row + 1, :] = source[:, row * LANES : (row + 1) * LANES]
        row = source.shape[1] // LANES
        sums.small[index, row : row + 1, :] = r.router_grad[...]
        sums.small[index, row + 1 : row + 2, :] = extra[...]
        left = sums.small.shape[1] - row - 2
        sums.small[index, row + 2 :, :] = jnp.zeros((left, LANES), F32)
    sums.small_begin()
    sums.show()

    for turn in range(max(sums.end - sums.now, sums.bits + 1)):
        if sums.now < sums.end:
            sums.moment()
        if turn <= sums.bits:
            sums.small_turn(turn)
    sums.close()


def layer_body(r, groups, window, full, is_router):
    def hook(at):
        if at in r.hooks:
            r.hooks[at]()

    rows, width = r.x.shape
    hidden = r.own[2].shape[2]
    pairs = width // 128
    row_tile = rows // 5

    def vec(start, count=width):
        return r.vec[:, start : start + count]

    g1, g2, b1, bq, bv, bo, b2 = (vec(k * width) for k in range(7))
    bu_at, bd_at = 7 * width, 7 * width + hidden

    def row_loop(step, init=0):
        def at(k, carry):
            return step(pl.ds(pl.multiple_of(k * row_tile, row_tile), row_tile), carry)

        return lax.fori_loop(0, rows // row_tile, at, init)

    def norm_step(source, gain, bias, target):
        def step(here, carry):
            normal, _ = norm_stats(source[here, :].astype(F32))
            target[here, :] = (normal * gain + bias).astype(BF16)
            return carry

        return step

    def tiles(step):
        for k in range(width // STEP):
            step(slice(k * STEP, (k + 1) * STEP))

    def show(source, target):
        def step(span):
            target[:, span] = dot(r.unsort[...], source[:, span]).astype(BF16)

        tiles(step)

    def spread(routed, others, target, shown):
        def step(span):
            value = dot(r.unpick[...], routed[:, span]) + others[:, span].astype(F32) * r.skipped[...]
            if target is not None:
                target[:, span] = value.astype(BF16)
            shown[:, span] = dot(r.unsort[...], value.astype(BF16)).astype(BF16)

        tiles(step)

    row_loop(norm_step(r.x, g1, b1, r.n1))
    if full and is_router:

        def route_step(span):
            r.dout[:, span] = dot(r.pick[...], r.all_dout[:, span]).astype(BF16)

        tiles(route_step)
    if full:

        def delta_step(here, carry):
            low = r.dout[here, :]
            if is_router:
                low = (low.astype(F32) * r.scale[here, :]).astype(BF16)
                r.dmlp[here, :] = low
            return carry + fold(low.astype(F32))

        dbd = row_loop(delta_step, jnp.zeros((8, width), F32))
        r.small[:, bd_at:] = jnp.sum(dbd, axis=0, keepdims=True)

    for k, (start, low, high) in enumerate(groups):
        col = r.col_code[start : start + window, :]
        row = r.row_code[:, start : start + window]
        place = lax.broadcasted_iota(jnp.int32, (window, 1), 0) + start
        col = jnp.where((place >= low) & (place < high), col, -1)
        r.mask[k] = jnp.where(col == row, 0.0, NEGATIVE)

    r.ready(0)
    for k in range(3 * width // STEP):
        span = slice(k * STEP, (k + 1) * STEP)
        value = dot(r.n1[...], r.weights[0][:, span])
        if k < width // STEP:
            value = (value + bq[:, span]).astype(BF16).astype(F32) * 0.125
        elif k >= 2 * width // STEP:
            value = value + bv[:, k * STEP - 2 * width : (k + 1) * STEP - 2 * width]
        r.qkv[:, span] = value.astype(BF16)

    hook(0)
    lane = lax.broadcasted_iota(jnp.int32, (1, 128), 1)

    def halves(block):
        zero = jnp.zeros_like(block)
        return jnp.concatenate([jnp.where(lane < 64, block, zero), jnp.where(lane < 64, zero, block)], axis=0)

    high_half = lax.broadcasted_iota(jnp.int32, (128, 1), 0) >= 64

    def own_half(both):
        return jnp.where(high_half, both[:, window:], both[:, :window]).T

    r.mix[...] = jnp.zeros_like(r.mix)

    def lanes(pair, part):
        return pl.ds(pl.multiple_of(pair * 128 + part * width, 128), 128)

    spots = [slice(start, start + window) for start, _, _ in groups]
    count = len(groups)

    def qkv_at(pair, part):
        return [r.qkv[here, lanes(pair, part)] for here in spots]

    def attend(pair, carry):
        q, key, v = (qkv_at(pair, part) for part in range(3))
        scores = [dot(key[k], halves(q[k]), NT) for k in range(count)]
        probs = []
        for k, (start, low, high) in enumerate(groups):
            mask = r.mask[k]
            masked = scores[k] + jnp.concatenate([mask, mask], axis=1)
            place = lax.broadcasted_iota(jnp.int32, (1, window), 1) + start
            valid = (place >= low) & (place < high)
            valid = jnp.concatenate([valid, valid], axis=1)
            power = jnp.exp(masked - jnp.max(masked, axis=0, keepdims=True))
            total = jnp.sum(power, axis=0, keepdims=True)
            prob = (power * jnp.where(valid, 1.0 / total, 0.0)).astype(BF16)
            if full:
                r.probs[pair * count + k] = prob
            probs.append(prob)
        mixed = [dot(v[k].T, probs[k]) for k in range(count)]
        for k, here in enumerate(spots):
            r.mix[here, lanes(pair, 0)] = r.mix[here, lanes(pair, 0)] + own_half(mixed[k]).astype(BF16)
        return carry

    lax.fori_loop(0, pairs, attend, 0)

    r.ready(1)
    for k in range(width // STEP):
        span = slice(k * STEP, (k + 1) * STEP)
        value = dot(r.mix[...], r.weights[1][:, span]) + bo[:, span]
        r.between[:, span] = r.x[:, span].astype(F32) + value
    row_loop(norm_step(r.between, g2, b2, r.n2))
    if full:
        r.n1t[...] = r.n1[...].T
        r.n2t[...] = r.n2[...].T
    hook(1)

    r.ready(2)
    if full:
        r.ready(3)

    def down_out(k, slot):
        r.tile_out(
            r.down_stage.at[slot], pl.multiple_of(k * STEP, STEP), 0, (STEP, width), r.down_sem.at[slot], k
        )

    def side_out(block, k, slot):
        row = pl.multiple_of((block + k // 3) * width, width)
        column = pl.multiple_of(k % 3 * STEP, STEP)
        tile = k + {4: 12, 8: 24, 9: 27}[block]
        r.tile_out(r.up_stage.at[slot], row, column, (width, STEP), r.up_sem.at[slot], tile)

    def down_free(slot):
        target = r.grads.at[pl.ds(0, STEP), pl.ds(0, width)]
        pltpu.make_async_copy(r.down_stage.at[slot], target, r.down_sem.at[slot]).wait()

    def side_free(slot):
        target = r.grads.at[pl.ds(0, width), pl.ds(0, STEP)]
        pltpu.make_async_copy(r.up_stage.at[slot], target, r.up_sem.at[slot]).wait()

    steps = hidden // STEP

    def part_at(k):
        return pl.multiple_of(k * STEP, STEP)

    def ahead(k, side):
        at = part_at(k)
        r.pre[side][...] = dot(r.n2[...], r.weights[2][:, pl.ds(at, STEP)]) + r.vec[:, pl.ds(at + bu_at, STEP)]

    def middle(k, side):
        at = part_at(k)
        span = pl.ds(at, STEP)
        pre = r.pre[side][...]
        cdf, bell = gelu_parts(pre)
        act = (pre * cdf).astype(BF16)
        if not (full and is_router):
            r.act[:, span] = act
        if full:
            r.act_part[side][...] = act
            slope = cdf + pre * bell * 0.3989422804014327
            dact = dot(r.dmlp[...], r.weights[3][span, :], NT)
            dpre = (dact * slope).astype(BF16)
            r.dpre[:, span] = dpre
            r.dpre_part[side][...] = dpre
            r.small[:, pl.ds(at + bu_at, STEP)] = jnp.sum(dpre.astype(F32), axis=0, keepdims=True)

    def weigh(side):
        r.down_stage[side] = dot(r.act_part[side][...], r.dmlp[...], TN).astype(BF16)
        r.up_stage[side] = dot(r.n2t[...], r.dpre_part[side][...]).astype(BF16)

    def send_out(k, side):
        down_out(k, side)
        side_out(4, k, side)

    def two_steps(kk, first=False):
        even, odd = kk, kk + steps // 2
        if full and not first:

            @pl.when(kk >= 2)
            def _():
                down_free(1)
                side_free(1)

            down_free(0)
            side_free(0)
        middle(even, 0)
        ahead(odd, 1)
        if full and not first:
            weigh(1)
        middle(odd, 1)
        ahead(jnp.minimum(even + 1, steps // 2 - 1), 0)
        if full:
            weigh(0)
            if not first:
                send_out(odd - 1, 1)
            send_out(even, 0)

    def more_steps(kk, carry):
        two_steps(kk)
        return carry

    ahead(0, 0)
    two_steps(0, True)
    if 2 in r.hooks:
        lax.fori_loop(1, steps // 4, more_steps, 0)
        hook(2)
        lax.fori_loop(steps // 4, steps // 2, more_steps, 0)
    else:
        lax.fori_loop(1, steps // 2, more_steps, 0)
    if full:
        down_free(1)
        side_free(1)
        weigh(1)
        send_out(steps - 1, 1)
        for side in range(2):
            down_free(side)
            side_free(side)
        hook(3)
    if not full:
        r.ready(3)
    if not (full and is_router):
        for k in range(width // STEP):
            span = slice(k * STEP, (k + 1) * STEP)
            value = dot(r.act[...], r.weights[3][:, span]) + vec(bd_at)[:, span]
            source = r.x[:, span].astype(F32)
            value = r.between[:, span] - source + value
            if not full:
                r.delta[:, span] = value
            r.y[:, span] = (source + (r.scale[...] * value if is_router else value)).astype(BF16)
    if not full:
        spread(r.y, r.all_x, r.all_y, r.shown_y)
        return
    if not is_router:
        show(r.y, r.shown_du)
        r.shown_copy = pltpu.make_async_copy(r.shown_du, r.shown_y, r.shown_sem.at[0])
        r.shown_copy.start()

    r.dn[...] = dot(r.dpre[...], r.weights[2][...], NT)
    hook(4)

    def norm_back(source, gain, here):
        normal, recip = norm_stats(source[here, :].astype(F32))
        grad = r.dn[here, :]
        hat = grad * gain
        back = recip * (
            hat - jnp.mean(hat, axis=-1, keepdims=True) - normal * jnp.mean(hat * normal, axis=-1, keepdims=True)
        )
        return back, fold(grad * normal), fold(grad)

    def second_back(here, carry):
        back, dg, db = norm_back(r.between, g2, here)
        r.between[here, :] = back
        delta = r.dout[here, :].astype(F32)
        total = ((delta * r.scale[here, :] if is_router else delta) + back).astype(BF16)
        r.datt[here, :] = total
        return carry[0] + dg, carry[1] + db, carry[2] + fold(total.astype(F32))

    zero = jnp.zeros((8, width), F32)
    dg2, db2, dbo = row_loop(second_back, (zero, zero, zero))
    r.small[:, width : 2 * width] = jnp.sum(dg2, axis=0, keepdims=True)
    r.small[:, 6 * width : 7 * width] = jnp.sum(db2, axis=0, keepdims=True)
    r.small[:, 5 * width : 6 * width] = jnp.sum(dbo, axis=0, keepdims=True)

    hook(5)
    r.mixt[...] = r.mix[...].T
    r.dmix[...] = dot(r.datt[...], r.weights[1][...], NT).astype(BF16)
    for k in range(width // STEP):
        span = slice(k * STEP, (k + 1) * STEP)
        slot = k % 2
        if k >= 2:
            side_free(slot)
        r.up_stage[slot] = dot(r.mixt[...], r.datt[:, span]).astype(BF16)
        side_out(8, k, slot)
    hook(6)

    r.dqkv[...] = jnp.zeros((rows, 3 * width), BF16)

    def attend_back(pair, carry):
        q, key, v = (qkv_at(pair, part) for part in range(3))
        dm = [halves(r.dmix[here, lanes(pair, 0)]) for here in spots]
        dprobs = [dot(v[k], dm[k], NT) for k in range(count)]
        dv = [dot(r.probs[pair * count + k], dm[k]) for k in range(count)]
        ds = []
        for k in range(count):
            wide = r.probs[pair * count + k].astype(F32)
            product = wide * dprobs[k]
            ds.append((product - wide * jnp.sum(product, axis=0, keepdims=True)).astype(BF16))
        dk = [dot(ds[k], halves(q[k])) for k in range(count)]
        dq = [dot(key[k].T, ds[k]) for k in range(count)]
        for k, here in enumerate(spots):
            for part, value in enumerate((own_half(dq[k]) * 0.125, dk[k], dv[k])):
                spot = lanes(pair, part)
                r.dqkv[here, spot] = r.dqkv[here, spot] + value.astype(BF16)
        return carry

    if 7 in r.hooks:
        lax.fori_loop(0, pairs // 2, attend_back, 0)
        hook(7)
        lax.fori_loop(pairs // 2, pairs, attend_back, 0)
    else:
        lax.fori_loop(0, pairs, attend_back, 0)
    hook(8)

    for k in range(3 * width // STEP):
        span = slice(k * STEP, (k + 1) * STEP)
        block = r.dqkv[:, span]
        if not width <= k * STEP < 2 * width:
            at = 3 * width + k * STEP - (width if k * STEP >= width else 0)
            r.small[:, at : at + STEP] = jnp.sum(block.astype(F32), axis=0, keepdims=True)
        slot = (k + 1) % 2
        side_free(slot)
        r.up_stage[slot] = dot(r.n1t[...], block).astype(BF16)
        side_out(9, k, slot)
    side_free(0)
    side_free(1)
    hook(9)

    r.dn[...] = dot(r.dqkv[...], r.weights[0][...], NT)

    def first_back(here, carry):
        back, dg, db = norm_back(r.x, g1, here)
        dout = r.dout[here, :].astype(F32)
        total = dout + r.between[here, :] + back
        sums = [carry[0] + dg, carry[1] + db]
        if is_router:
            slope = jnp.sum(dout * r.delta[here, :], axis=1, keepdims=True) * r.factor[here, :]
            total = total + slope * r.router[...]
            sums.append(carry[2] + fold(slope * r.x[here, :].astype(F32)))
        r.du[here, :] = total.astype(BF16)
        return tuple(sums)

    sums = row_loop(first_back, (zero,) * (3 if is_router else 2))
    r.small[:, :width] = jnp.sum(sums[0], axis=0, keepdims=True)
    r.small[:, 2 * width : 3 * width] = jnp.sum(sums[1], axis=0, keepdims=True)
    if is_router:
        r.router_grad[...] = jnp.sum(sums[2], axis=0, keepdims=True)
        spread(r.du, r.all_dout, None, r.shown_du)
    else:
        r.shown_copy.wait()
        show(r.du, r.shown_du)


def front_scratch(rows, width, hidden, groups, window, full, keep_act):
    sizes = [(width, 3 * width), (width, width), (width, hidden), (hidden, width)]
    held = [pltpu.VMEM(size, BF16) for size in sizes]
    held += [pltpu.SemaphoreType.DMA((4,))]
    held += [pltpu.VMEM((rows, width), BF16), pltpu.VMEM((rows, 3 * width), BF16)]
    held += [pltpu.VMEM((HEADS // 2 * len(groups) if full else 1, window, 2 * window), BF16)]
    held += [pltpu.VMEM((len(groups), window, window), F32), pltpu.VMEM((rows, width), BF16)]
    held += [pltpu.VMEM((rows, width), F32), pltpu.VMEM((rows, width), BF16)]
    held += [pltpu.VMEM((rows, hidden) if keep_act else (TILE, LANES), BF16)]
    held += [pltpu.VMEM((rows, STEP), F32)] * (0 if full else 2)
    return held + [pltpu.VMEM((rows, STEP), BF16)] * 2


def back_scratch(rows, width, hidden, scaled):
    held = [pltpu.VMEM((width, rows), BF16)] * 2 + [pltpu.VMEM((rows, width), BF16)] * int(scaled)
    held += [pltpu.VMEM((rows, hidden), BF16), pltpu.VMEM((rows, width), F32)]
    held += [pltpu.VMEM((rows, STEP), BF16)] * 2
    held += [pltpu.VMEM((2, STEP, width), BF16), pltpu.VMEM((2, width, STEP), BF16)]
    return held + [pltpu.SemaphoreType.DMA((2,))] * 2


def run_start(groups, window, lengths, route_mask, tokens, cotangent, router_row, own_vec, own):
    _, rows, width = tokens.shape
    half, hidden = rows // 2, own[2].shape[2]
    inside = pl.BlockSpec(memory_space=pltpu.VMEM)
    anywhere = pl.BlockSpec(memory_space=pl.ANY)
    outs = [(value.shape, BF16) for value in own] + [(own_vec.shape, F32)] * 2
    outs += [((rows, width), BF16)] * 2 + [((half, width), F32), ((rows, width), BF16), ((half, width), BF16)]
    outs += [((half, 1), jnp.int32), ((rows, 1), jnp.int32), ((1, half), jnp.int32), ((1, rows), jnp.int32)]
    outs += [((rows, rows), BF16), ((half, rows), BF16), ((rows, half), BF16), ((rows, 1), F32)]
    outs += [((half, 1), F32)] * 2 + [((1, width), F32)]
    scratch = front_scratch(half, width, hidden, groups, window, False, True)
    scratch += [pltpu.VMEM((half, width), BF16), pltpu.VMEM((rows, width), BF16), pltpu.VMEM((rows, rows), BF16)]
    scratch += [pltpu.VMEM((2, rows, width), BF16), pltpu.VMEM(own_vec.shape, F32), pltpu.SemaphoreType.DMA((2,))]
    scratch += [pltpu.SemaphoreType.DMA((4,))] * 2 + [pltpu.SemaphoreType.DMA((2,))]
    return pl.pallas_call(
        functools.partial(start_kernel, groups, window),
        out_shape=[jax.ShapeDtypeStruct(*one) for one in outs],
        in_specs=[pl.BlockSpec(memory_space=pltpu.SMEM), inside] + [anywhere] * 2 + [inside] * 2 + [anywhere] * 4,
        out_specs=[anywhere] * 4 + [inside] * (len(outs) - 4),
        scratch_shapes=scratch,
        compiler_params=pltpu.CompilerParams(
            collective_id=1, has_side_effects=True, vmem_limit_bytes=60 * 1024 * 1024
        ),
        cost_estimate=pl.CostEstimate(flops=5 * 10**9, bytes_accessed=6 * 10**7, transcendentals=0),
        name="start",
    )(lengths, route_mask, tokens, cotangent, router_row, own_vec, *own)


def run_layer(axis_of, groups, window, x, col_code, row_code, vec, own, far, unsort, back):
    chunks = sum_plan(axis_of)
    reduced = len(REDUCED)
    rows, width = x.shape
    hidden = own[2].shape[2]
    inside = pl.BlockSpec(memory_space=pltpu.VMEM)
    anywhere = pl.BlockSpec(memory_space=pl.ANY)
    args = [x, col_code, row_code, vec, *own, *far, unsort, back]
    outs = [((rows, width), BF16), ((1, vec.shape[1]), F32), ((GRAD_ROWS, LANES), BF16)]
    outs += [((rows, width), BF16)] * 2 + [((GRAD_ROWS, LANES), BF16), ((reduced * GROUP_ROWS, LANES), BF16)]
    scratch = front_scratch(rows, width, hidden, groups, window, True, True)
    scratch += back_scratch(rows, width, hidden, False) + [pltpu.SemaphoreType.DMA((1,))]
    scratch += Sums.scratch(chunks, reduced, 0)
    flops = rows * width * (3 * width + width + 2 * hidden) * 6
    return pl.pallas_call(
        functools.partial(layer_kernel, groups, window, chunks),
        out_shape=[jax.ShapeDtypeStruct(*one) for one in outs],
        in_specs=[inside] * 4 + [anywhere] * 8 + [inside] * 2,
        out_specs=[inside] * 2 + [anywhere] + [inside] + [anywhere] * 3,
        scratch_shapes=scratch,
        compiler_params=pltpu.CompilerParams(
            collective_id=2, has_side_effects=True, vmem_limit_bytes=64 * 1024 * 1024
        ),
        cost_estimate=pl.CostEstimate(flops=flops, bytes_accessed=3 * 10**7, transcendentals=0),
        name="layer",
    )(*args)


def run_fused(axis_of, groups, window, x, col_code, row_code, vec, scale, own, far, rows_of, back, router, second, extra, shown):
    rows, width = x.shape
    hidden = own[2].shape[2]
    chunks = sum_plan(axis_of)
    inside = pl.BlockSpec(memory_space=pltpu.VMEM)
    anywhere = pl.BlockSpec(memory_space=pl.ANY)
    unsort, pick, unpick, skipped = rows_of
    delta, factor, router_row = router
    every = unsort.shape[0]
    args = [x, col_code, row_code, vec, scale, *own, *far, unsort]
    args += [back, pick, unpick, skipped, delta, factor, router_row]
    args += [*second, extra, *shown]
    small_rows = -(-(vec.shape[1] // LANES + 2) // 8) * 8
    outs = [((GRAD_ROWS, LANES), BF16)] * 4
    outs += [((small_rows, LANES), F32)] + [((2, every, width), BF16)] * 2
    scratch = front_scratch(rows, width, hidden, groups, window, True, False)
    scratch += back_scratch(rows, width, hidden, True)
    scratch += [pltpu.VMEM((rows, width), BF16)] * 2 + [pltpu.VMEM((every, width), BF16)]
    scratch += [pltpu.VMEM((1, vec.shape[1]), F32), pltpu.VMEM((1, width), F32)]
    scratch += Sums.scratch(chunks, GROUPS, small_rows)
    *sums, _, _, small, acts, grads = pl.pallas_call(
        functools.partial(fused_kernel, groups, window, chunks),
        out_shape=[jax.ShapeDtypeStruct(*one) for one in outs],
        in_specs=[inside] * 5 + [anywhere] * 8 + [inside] * 8 + [anywhere] * 3 + [inside] * 2 + [anywhere] * 3,
        out_specs=[anywhere] * 4 + [inside] + [anywhere] * 2,
        scratch_shapes=scratch,
        compiler_params=pltpu.CompilerParams(
            collective_id=0, has_side_effects=True, vmem_limit_bytes=64 * 1024 * 1024
        ),
        cost_estimate=pl.CostEstimate(flops=10**10, bytes_accessed=6 * 10**8, transcendentals=0),
        name="fused",
    )(*args)
    return sums, small, (acts, grads)


def body(axis_of, tokens, lengths, route_mask, router_weight, gains, biases, w_qkv, w_out, w_up, w_down, cotangent):
    micro, rows, width = tokens.shape
    own = (w_qkv, w_out, w_up, w_down)
    own_vec = jnp.concatenate([gains, biases], axis=1)
    router_row = router_weight.astype(F32)[None, :]
    half = LONG // 2
    groups_one = ((0, 0, half), (96, half, 2 * half), (192, 2 * half, rows // 2))
    groups_two = ((0, 0, LONG), (192, LONG, 2 * LONG), (384, 2 * LONG, rows))
    made = run_start(groups_one, 128, lengths, route_mask, tokens, cotangent, router_row, own_vec, own)
    far, (vec_one, vec_two), (y1, shown_y1, delta_one, cot, routed) = made[:4], made[4:6], made[6:11]
    col_one, col_two, row_one, row_two, *others = made[11:]
    unsort, pick, unpick, skipped, scale, factor, extra = others
    shown_du2, small_two, grads_two, dout, shown_y2, landed_two, carry = run_layer(
        axis_of, groups_two, 256, y1, col_two, row_two, vec_two, own, far, unsort, cot
    )
    sums, small, (activations, input_grads) = run_fused(
        axis_of, groups_one, 128, routed, col_one, row_one, vec_one, scale, own, far,
        (unsort, pick, unpick, skipped), dout, (delta_one, factor, router_row),
        (grads_two, landed_two, carry, small_two), extra,
        (shown_y1, shown_y2, shown_du2),
    )
    *grads, router_grad, means, activations, input_grads = cast_sums(
        sums, small, activations, input_grads,
        [value.shape for value in (*own, gains, biases)], micro,
    )
    return (activations, input_grads, *grads, router_grad[0], means[0])


def solution(mesh):
    in_specs = (
        P(None, "dp", None),
        P(None, "dp", None),
        P(None, "dp"),
        P(),
        P("section", None),
        P("section", None),
        P("section", None, None),
        P("section", None, None),
        P("section", None, None),
        P("section", None, None),
        P(None, "dp", None),
    )
    out_specs = (
        P("section", None, "dp", None),
        P("section", None, "dp", None),
        P("section", None, None),
        P("section", None, None),
        P("section", None, None),
        P("section", None, None),
        P("section", None),
        P("section", None),
        P(),
        P(),
    )
    step = functools.partial(body, axis_bits(mesh))
    return jax.shard_map(step, mesh=mesh, in_specs=in_specs, out_specs=out_specs, check_vma=False)
```

profile of v0, /device:TPU:0, one launch (start us, length us, event | category | flops | bytes accessed | tf_op | source)
XLA Modules:
  0.0 380.1 jit_solution(7982518987187732234)
XLA Ops:
  0.6 1.3 reshape.20.refs_4_.refs_20_
  1.9 1.4 pad_maximum_fusion.refs_5_
  3.3 26.1 %start.1 = (bf16[1,768,2304]{2,1,0:T(8,128)(2,1)}, bf16[1,768,768]{2,1,0:T(8,128)(2,1)}, bf16[1,768,3072]{2,1,0:T(8,128)(2,1)}, bf16[1,3072,768]{2,1,0:T(8,128)(...) custom-call(s32[2,1,8]{2,1,0:T(1,128)} %refs_0_.1, ...), custom_call_target="tpu_custom_call" | custom-call | flops 5000000000 | bytes 60000000 | tf_op jit(solution)/shard_map/start/pallas_call | solution.py:1166
  29.4 115.6 %layer.1 = (bf16[640,768]{1,0:T(8,128)(2,1)}, f32[1,9216]{1,0:T(1,128)}, bf16[9216,768]{1,0:T(8,128)(2,1)}, bf16[640,768]{1,0:T(8,128)(2,1)}, bf16[640,768]{1,0:...) custom-call(bf16[640,768]{1,0:T(8,128)(2,1)} %get-tuple-element.64.refs_0_, ...), custom_call_target="tpu_custom_call" | custom-call | flops 27179089920 | bytes 30000000 | tf_op jit(solution)/shard_map/layer/pallas_call | solution.py:1194
  145.0 216.0 %fused.1 = (bf16[9216,768]{1,0:T(8,128)(2,1)}, bf16[9216,768]{1,0:T(8,128)(2,1)}, bf16[9216,768]{1,0:T(8,128)(2,1)}, bf16[9216,768]{1,0:T(8,128)(2,1)}, f32[16,7...) custom-call(bf16[320,768]{1,0:T(8,128)(2,1)} %get-tuple-element.54.refs_0_, ...), custom_call_target="tpu_custom_call" | custom-call | flops 10000000000 | bytes 600000000 | tf_op jit(solution)/shard_map/fused/pallas_call | solution.py:1228
  361.1 17.5 %cast.1 = (f32[1,768,2304]{2,1,0:T(8,128)}, f32[1,768,768]{2,1,0:T(8,128)}, f32[1,768,3072]{2,1,0:T(8,128)}, f32[1,3072,768]{2,1,0:T(8,128)}, f32[1,1536]{1,0:T(...) custom-call(bf16[9216,768]{1,0:T(8,128)(2,1)} %get-tuple-element.83., ...), custom_call_target="tpu_custom_call" | custom-call | bytes 50000000 | tf_op jit(solution)/shard_map/cast/pallas_call | solution.py:459
  378.6 1.3 reduce
where the time goes:
time: 384 us; the launch traced here: 380 us
  Pallas kernels  375 us (98%)
    pallas_call x1, Pallas kernels, run_fused(): pl.pallas_call(functools.partial(fused_kernel, groups, window, chunks), o...  216 us
    pallas_call x1, Pallas kernels, run_layer(): pl.pallas_call(functools.partial(layer_kernel, groups, window, chunks), o...  116 us
    pallas_call x1, Pallas kernels, run_start(): pl.pallas_call(functools.partial(start_kernel, groups, window), out_shape...  26.1 us
    pallas_call x1, Pallas kernels, cast_sums(): pl.pallas_call(cast_kernel, out_shape=[jax.ShapeDtypeStruct(*one) for one...  17.5 us

commit v1 on v0

--- a/solution.py
+++ b/solution.py
@@ -157,7 +157,9 @@
         barrier = pltpu.get_barrier_semaphore()
         for friend in friends:
             pl.semaphore_signal(barrier, inc=1, device_id=friend, device_id_type=pl.DeviceIdType.MESH)
-        pl.semaphore_wait(barrier, len(friends))
+
+    def meet(self):
+        pl.semaphore_wait(pltpu.get_barrier_semaphore(), 1 + self.bits)
 
     @staticmethod
     def layer_of(j):
@@ -462,11 +464,11 @@
         in_specs=[anywhere] * 2 + [inside] + [anywhere] * 2,
         out_specs=[anywhere] * 4 + [inside] * 4 + [anywhere] * 2,
         scratch_shapes=[
-            pltpu.VMEM((4, LANES, LANES), BF16),
-            pltpu.VMEM((4, LANES, LANES), F32),
+            pltpu.VMEM((6, 256, LANES), BF16),
+            pltpu.VMEM((6, 256, LANES), F32),
             pltpu.VMEM((2, *acts.shape), BF16),
-            pltpu.SemaphoreType.DMA((4,)),
-            pltpu.SemaphoreType.DMA((4,)),
+            pltpu.SemaphoreType.DMA((6,)),
+            pltpu.SemaphoreType.DMA((6,)),
             pltpu.SemaphoreType.DMA((2,)),
         ],
         compiler_params=pltpu.CompilerParams(vmem_limit_bytes=60 * 1024 * 1024),
@@ -555,6 +557,7 @@
     sums.open()
     r.tile_out = functools.partial(sums.tile_out, 1)
     r.hooks = {at: sums.moment for at in (4, 7, 8)}
+    r.hooks[1] = sums.meet
     r.hooks[3] = lambda: sums.prepare(0)
     layer_body(r, groups, window, True, False)
     while sums.now < sums.end:
@@ -732,6 +735,7 @@
     r.grads = first
     use_weights(r, 0)
     sums.open()
+    sums.meet()
     for j in range(reduced):
         for c in sums.each(j):
             sums.carried(j, c, False).start()
@@ -1000,10 +1004,6 @@
         side_free(1)
         weigh(1)
         send_out(steps - 1, 1)
-        for side in range(2):
-            down_free(side)
-            side_free(side)
-        hook(3)
     if not full:
         r.ready(3)
     if not (full and is_router):
@@ -1023,6 +1023,10 @@
         r.shown_copy = pltpu.make_async_copy(r.shown_du, r.shown_y, r.shown_sem.at[0])
         r.shown_copy.start()
 
+    for side in range(2):
+        down_free(side)
+        side_free(side)
+    hook(3)
     r.dn[...] = dot(r.dpre[...], r.weights[2][...], NT)
     hook(4)
 
@@ -1099,8 +1103,9 @@
         side_free(slot)
         r.up_stage[slot] = dot(r.n1t[...], block).astype(BF16)
         side_out(9, k, slot)
-    side_free(0)
-    side_free(1)
+    if is_router:
+        side_free(0)
+        side_free(1)
     hook(9)
 
     r.dn[...] = dot(r.dqkv[...], r.weights[0][...], NT)
@@ -1126,6 +1131,8 @@
     else:
         r.shown_copy.wait()
         show(r.du, r.shown_du)
+        side_free(0)
+        side_free(1)
 
 
 def front_scratch(rows, width, hidden, groups, window, full, keep_act):

time: 384 us -> 381 us (level)
    pallas_call x1, Pallas kernels: 116 us -> 102 us  [run_layer(): pl.pallas_call(functools.partial(layer_kernel, groups, window, chunks), o...]
    pallas_call x1, Pallas kernels: 216 us -> 226 us  [run_fused(): pl.pallas_call(functools.partial(fused_kernel, groups, window, chunks), o...]
where the time goes in v1:
time: 381 us; the launch traced here: 377 us
  Pallas kernels  372 us (98%)
    pallas_call x1, Pallas kernels, run_fused(): pl.pallas_call(functools.partial(fused_kernel, groups, window, chunks), o...  226 us
    pallas_call x1, Pallas kernels, run_layer(): pl.pallas_call(functools.partial(layer_kernel, groups, window, chunks), o...  102 us
    pallas_call x1, Pallas kernels, run_start(): pl.pallas_call(functools.partial(start_kernel, groups, window), out_shape...  26.1 us
    pallas_call x1, Pallas kernels, cast_sums(): pl.pallas_call(cast_kernel, out_shape=[jax.ShapeDtypeStruct(*one) for one...  17.9 us

profile of v1, /device:TPU:0, one launch (start us, length us, event | category | flops | bytes accessed | tf_op | source)
XLA Modules:
  0.0 376.9 jit_solution(1007290723656446785)
XLA Ops:
  0.6 1.3 reshape.20.refs_4_.refs_20_
  1.9 1.4 pad_maximum_fusion.refs_5_
  3.3 26.1 %start.1 = (bf16[1,768,2304]{2,1,0:T(8,128)(2,1)}, bf16[1,768,768]{2,1,0:T(8,128)(2,1)}, bf16[1,768,3072]{2,1,0:T(8,128)(2,1)}, bf16[1,3072,768]{2,1,0:T(8,128)(...) custom-call(s32[2,1,8]{2,1,0:T(1,128)} %refs_0_.1, ...), custom_call_target="tpu_custom_call" | custom-call | flops 5000000000 | bytes 60000000 | tf_op jit(solution)/shard_map/start/pallas_call | solution.py:1173
  29.4 102.0 %layer.1 = (bf16[640,768]{1,0:T(8,128)(2,1)}, f32[1,9216]{1,0:T(1,128)}, bf16[9216,768]{1,0:T(8,128)(2,1)}, bf16[640,768]{1,0:T(8,128)(2,1)}, bf16[640,768]{1,0:...) custom-call(bf16[640,768]{1,0:T(8,128)(2,1)} %get-tuple-element.64.refs_0_, ...), custom_call_target="tpu_custom_call" | custom-call | flops 27179089920 | bytes 30000000 | tf_op jit(solution)/shard_map/layer/pallas_call | solution.py:1201
  131.4 226.1 %fused.1 = (bf16[9216,768]{1,0:T(8,128)(2,1)}, bf16[9216,768]{1,0:T(8,128)(2,1)}, bf16[9216,768]{1,0:T(8,128)(2,1)}, bf16[9216,768]{1,0:T(8,128)(2,1)}, f32[16,7...) custom-call(bf16[320,768]{1,0:T(8,128)(2,1)} %get-tuple-element.54.refs_0_, ...), custom_call_target="tpu_custom_call" | custom-call | flops 10000000000 | bytes 600000000 | tf_op jit(solution)/shard_map/fused/pallas_call | solution.py:1235
  357.5 17.9 %cast.1 = (f32[1,768,2304]{2,1,0:T(8,128)}, f32[1,768,768]{2,1,0:T(8,128)}, f32[1,768,3072]{2,1,0:T(8,128)}, f32[1,3072,768]{2,1,0:T(8,128)}, f32[1,1536]{1,0:T(...) custom-call(bf16[9216,768]{1,0:T(8,128)(2,1)} %get-tuple-element.83., ...), custom_call_target="tpu_custom_call" | custom-call | bytes 50000000 | tf_op jit(solution)/shard_map/cast/pallas_call | solution.py:461
  375.4 1.3 reduce
